TPU v7x, 32 devices: a whole 2x2x4 slice. The times are simulated.
32 devices in a mesh: stream: 4 (over y, x), blk: 8 (over z, core).
Axes of the slice: x: 2, y: 2, z: 4, core: 2. Of those that a mesh axis runs over, the one named last changes fastest.
Arguments:
- latents: bfloat16 [16384, 1152], P(('stream', 'blk')), may hold values from -6 to 6
- skip_input: bfloat16 [16384, 1152], P(('stream', 'blk')), may hold values from -6 to 6
- cond_tokens: bfloat16 [64, 2, 1152], P('stream'), may hold values from -6 to 6
- extra_length: int32 [4, 16], P('stream'), may hold values from 1 to 129, 1040 in all within a row
- skip_weight: bfloat16 [2304, 1152], P('blk'), may hold values from -0.125 to 0.125
- skip_bias: bfloat16 [1152], P('blk'), may hold values from -1.75 to 1.75
- first_gain: bfloat16 [1152], P('blk'), may hold values from 0.25 to 1.75
- first_shift: bfloat16 [1152], P('blk'), may hold values from -1.75 to 1.75
- joint_weight: bfloat16 [1152, 3456], P('blk'), may hold values from -0.1875 to 0.1875
- out_weight: bfloat16 [1152, 1152], P('blk'), may hold values from -1.5 to 1.5
- out_bias: bfloat16 [1152], P('blk'), may hold values from -1.75 to 1.75
- second_gain: bfloat16 [1152], P('blk'), may hold values from 0.25 to 1.75
- second_shift: bfloat16 [1152], P('blk'), may hold values from -1.75 to 1.75
- up_weight: bfloat16 [1152, 4608], P('blk'), may hold values from -0.1875 to 0.1875
- up_bias: bfloat16 [4608], P('blk'), may hold values from -1.75 to 1.75
- down_weight: bfloat16 [4608, 1152], P('blk'), may hold values from -0.09375 to 0.09375
- down_bias: bfloat16 [1152], P('blk'), may hold values from -1.75 to 1.75
- cotangent: bfloat16 [16384, 1152], P(('stream', 'blk')), may hold values from -6 to 6
Outputs:
- output_tokens: bfloat16 [16384, 1152], P(('stream', 'blk'))
- latents_grad: bfloat16 [16384, 1152], P(('stream', 'blk'))
- skip_grad: bfloat16 [16384, 1152], P(('stream', 'blk'))
- cond_grad: bfloat16 [64, 2, 1152], P('stream')
- grad_skip_weight: float32 [2304, 1152], P('blk')
- grad_skip_bias: float32 [1152], P('blk')
- grad_first_gain: float32 [1152], P('blk')
- grad_first_shift: float32 [1152], P('blk')
- grad_joint_weight: float32 [1152, 3456], P('blk')
- grad_out_weight: float32 [1152, 1152], P('blk')
- grad_out_bias: float32 [1152], P('blk')
- grad_second_gain: float32 [1152], P('blk')
- grad_second_shift: float32 [1152], P('blk')
- grad_up_weight: float32 [1152, 4608], P('blk')
- grad_up_bias: float32 [4608], P('blk')
- grad_down_weight: float32 [4608, 1152], P('blk')
- grad_down_bias: float32 [1152], P('blk')
Inputs may be any that keep to these rules, and one draw needn't show every extreme that they name: In each stream the item lengths extra_length + 191 sum to 4096, and one item has exactly 320 tokens.
All inputs are finite; a program needn't handle non-finite values.
Results may differ from a plain program's by a relative error of at most 0.02.
Values may be sent and summed in bfloat16 or wider, within the bound.
A program may use at most 256 MiB of HBM per device.

v0:
```python
import functools
from functools import partial

import jax
import jax.numpy as jnp
from jax import lax
from jax.experimental import pallas as pl
from jax.experimental.pallas import tpu as pltpu
from jax.sharding import PartitionSpec as P

HEADS = 16
HEAD = 72
LEN_MIN = 192

MESH = pl.DeviceIdType.MESH
ANY = pl.BlockSpec(memory_space=pl.ANY)
WIDTH = 1152
PART = 144
SMALL = (16, 256)


class Place:
    def __init__(self):
        self.s = lax.axis_index("stream")
        self.b = lax.axis_index("blk")
        self.x = lax.rem(self.s, 2)
        self.y = lax.div(self.s, 2)
        self.c = lax.rem(self.b, 2)
        self.zz = lax.div(self.b, 2)

    def other(self, k):
        low, high = lax.rem(self.zz, 2), lax.div(self.zz, 2)
        return 2 * (1 - high if k & 2 else high) + (1 - low if k & 1 else low)

    def source(self, k):
        zz = self.zz
        table = ((1, 0, 3, 2), (2, 2, 1, 1), (3, 3, 0, 0))[k - 1]
        return jnp.where(zz < 2, jnp.where(zz == 0, table[0], table[1]), jnp.where(zz == 2, table[2], table[3]))

    def at(self, x=None, y=None, zz=None, c=None):
        x = self.x if x is None else x
        y = self.y if y is None else y
        zz = self.zz if zz is None else zz
        c = self.c if c is None else c
        return (2 * y + x, 2 * zz + c)


def greet(place):
    barrier = pltpu.get_barrier_semaphore()
    p = place
    near = [p.at(x=1 - p.x), p.at(y=1 - p.y), p.at(c=1 - p.c)] + [p.at(zz=p.other(k)) for k in (1, 2, 3)]
    for device in near:
        pl.semaphore_signal(barrier, inc=1, device_id=device, device_id_type=MESH)
    up = (p.c == 1) & (p.zz < 3)
    down = (p.c == 0) & (p.zz > 0)
    for go, device in ((up, (p.s, p.b + 1)), (down, (p.s, p.b - 1))):

        @pl.when(go)
        def _():
            pl.semaphore_signal(barrier, inc=1, device_id=device, device_id_type=MESH)

    pl.when(up | down)(lambda: pl.semaphore_wait(barrier, len(near) + 1))
    pl.when(jnp.logical_not(up | down))(lambda: pl.semaphore_wait(barrier, len(near)))


def remote(src, dst, send, recv, device):
    return pltpu.make_async_remote_copy(
        src_ref=src, dst_ref=dst, send_sem=send, recv_sem=recv, device_id=device, device_id_type=MESH
    )


def block(t, ref, b):
    if t in (1, 2):
        return ref.at[b]
    size = 2 if t == 0 else 4
    return ref.at[pl.ds(b * size, size)]


def piece(t, ref, b, x, y):
    if t in (1, 2):
        return ref.at[b, :, pl.ds(pl.multiple_of((2 * y + x) * WIDTH, 128), WIDTH)]
    if t == 3:
        return ref.at[4 * b + 2 * y + x]
    low, size = (0, 80) if y == 0 else (80, 64)
    return ref.at[2 * b + x, pl.ds(low, size)]


KINDS = ("half", "cols", "cols", "rows")


class Gather:
    SEMS = [pltpu.SemaphoreType.DMA((4, 6, 4, 2)), pltpu.SemaphoreType.DMA((12,)), pltpu.SemaphoreType.DMA((2, 8))]

    def __init__(self, place, shards, outs, scratch):
        self.place = place
        self.small_in, self.skip_in, self.joint_in, self.out_in, self.up_in, self.down_in = shards
        self.small = outs[0]
        self.outs = outs[1:]
        self.sems, self.local_sems, self.small_sems = scratch[:3]
        self.stage = scratch[3:]

    def copy(self, t, x, y, zz, c, stage, k, device):
        ref = piece(t, self.outs[t], 2 * zz + c, x, y)
        return remote(ref, ref, self.sems.at[t, stage, k, 0], self.sems.at[t, stage, k, 1], device)

    def each_y(self, t, run):
        if KINDS[t] != "half":
            run(self.place.y)
            return
        for value in (0, 1):
            pl.when(self.place.y == value)(lambda value=value: run(value))

    STAGE = [
        pltpu.VMEM((2, PART, WIDTH), jnp.bfloat16),
        pltpu.VMEM((PART, 4 * WIDTH), jnp.bfloat16),
        pltpu.VMEM((PART, 4 * WIDTH), jnp.bfloat16),
        pltpu.VMEM((4, PART, WIDTH), jnp.bfloat16),
    ]

    def locals(self, t):
        if t == 1:
            return [
                (self.joint_in, self.stage[1].at[:, pl.ds(0, 3 * WIDTH)]),
                (self.out_in, self.stage[1].at[:, pl.ds(3 * WIDTH, WIDTH)]),
            ]
        return [({0: self.skip_in, 2: self.up_in, 3: self.down_in}[t], self.stage[t])]

    def own_start(self, t):
        for i, (src, dst) in enumerate(self.locals(t)):
            pltpu.make_async_copy(src, dst, self.local_sems.at[2 * t + i]).start()

    def own_keep(self, t):
        return pltpu.make_async_copy(self.stage[t], block(t, self.outs[t], self.place.b), self.local_sems.at[8 + t])

    def own_done(self, t):
        for i, (src, dst) in enumerate(self.locals(t)):
            pltpu.make_async_copy(src, dst, self.local_sems.at[2 * t + i]).wait()
        self.own_keep(t).start()

    def own_copy(self, t, c):
        ref = block(t, self.outs[t], 2 * self.place.zz + c)
        src = self.stage[t]
        sems = self.sems.at[t, 4, 0]
        return remote(src, ref, sems.at[0], sems.at[1], self.place.at(c=1 - self.place.c))

    def small_copy(self, i, src, dst, device):
        return remote(src, dst, self.small_sems.at[0, i], self.small_sems.at[1, i], device)

    def small_start(self):
        p = self.place
        for i, device in enumerate([p.at(zz=p.other(k)) for k in (1, 2, 3)] + [p.at(c=1 - p.c)]):
            self.small_copy(i, self.small_in, self.small.at[p.b], device).start()

    def small_pass(self):
        p = self.place
        for i, k in enumerate((1, 2, 3)):
            ref = self.small.at[2 * p.other(k) + p.c]
            self.small_copy(i, ref, ref, p.at()).wait_recv()
            self.small_copy(4 + i, ref, ref, p.at(c=1 - p.c)).start()

    def small_done(self):
        p = self.place
        for i, k in enumerate((0, 1, 2, 3)):
            ref = self.small.at[2 * p.other(k) + 1 - p.c]
            self.small_copy(3 + i, ref, ref, p.at()).wait_recv()
        for i in range(7):
            self.small_copy(i, self.small_in, self.small_in, p.at()).wait_send()

    def stage_piece(self, t, y):
        x = self.place.x
        if t in (1, 2):
            return self.stage[t].at[:, pl.ds(pl.multiple_of((2 * y + x) * WIDTH, 128), WIDTH)]
        if t == 3:
            return self.stage[t].at[2 * y + x]
        low, size = (0, 80) if y == 0 else (80, 64)
        return self.stage[t].at[x, pl.ds(low, size)]

    def z_copies(self, t, y, zz, start, own=False):
        p = self.place
        for step, send in ((1, 0), (-1, 5)):
            go = (zz <= p.zz) & (p.zz < 3) if step == 1 else (zz >= p.zz) & (p.zz > 0)
            ref = piece(t, self.outs[t], 2 * zz + p.c, p.x, y)

            @pl.when(go)
            def _():
                copy = remote(self.stage_piece(t, y) if own else ref, ref, self.sems.at[t, send, zz, 0], self.sems.at[t, 0, zz, 1], p.at(zz=p.zz + step))
                copy.start() if start else copy.wait_send()

    def z_start(self, t):
        p = self.place
        self.each_y(t, lambda y: self.z_copies(t, y, p.zz, True, True))
        self.own_copy(t, p.c).start()

    def z_wait(self, t, y, zz):
        p = self.place
        self.copy(t, p.x, y, zz, p.c, 0, zz, p.at()).wait_recv()

    def z_done(self, t, k):
        p = self.place
        zz = p.source(k)

        def run(y):
            self.z_wait(t, y, zz)
            self.z_copies(t, y, zz, True)

        pl.when((p.zz > 0) & (p.zz < 3))(lambda: self.each_y(t, run))

    def xy_start(self, t, k):
        p = self.place
        zz = p.source(k)

        def run(y):
            pl.when((p.zz == 0) | (p.zz == 3))(lambda: self.z_wait(t, y, zz))
            self.copy(t, p.x, y, zz, p.c, 1, k, p.at(x=1 - p.x)).start()
            self.copy(t, p.x, y, zz, p.c, 2, k, p.at(y=1 - p.y)).start()

        self.each_y(t, run)

    def by_x(self, t, k):
        return k == 1 or (k == 2 and t % 2 == 0)

    def xy_done(self, t, k):
        p = self.place

        def run(y):
            zz = p.source(k)
            self.copy(t, 1 - p.x, y, zz, p.c, 1, k, p.at()).wait_recv()
            if self.by_x(t, k):
                self.copy(t, 1 - p.x, y, zz, p.c, 3, k, p.at(y=1 - p.y)).start()
            self.copy(t, p.x, 1 - y, zz, p.c, 2, k, p.at()).wait_recv()
            if not self.by_x(t, k):
                self.copy(t, p.x, 1 - y, zz, p.c, 3, k, p.at(x=1 - p.x)).start()

        self.each_y(t, run)

    def diag_done(self, t, k):
        p = self.place

        def run(y):
            zz = p.source(k)
            self.copy(t, 1 - p.x, 1 - y, zz, p.c, 3, k, p.at()).wait_recv()

        self.each_y(t, run)
        self.pair_copy(t, k, p.c).start()

    def pair_copy(self, t, k, c):
        ref = block(t, self.outs[t], 2 * self.place.source(k) + c)
        sems = self.sems.at[t, 4, k]
        return remote(ref, ref, sems.at[0], sems.at[1], self.place.at(c=1 - self.place.c))

    def ready(self, t):
        p = self.place
        self.own_keep(t).wait()
        self.own_copy(t, 1 - p.c).wait_recv()
        for k in (1, 2, 3):
            self.pair_copy(t, k, 1 - p.c).wait_recv()

    def all_sent(self, t):
        p = self.place
        self.own_copy(t, p.c).wait_send()

        def run(y):
            self.z_copies(t, y, p.zz, False, True)
            for k in (1, 2, 3):
                zz = p.source(k)
                self.z_copies(t, y, zz, False)
                self.copy(t, p.x, y, zz, p.c, 1, k, p.at()).wait_send()
                self.copy(t, p.x, y, zz, p.c, 2, k, p.at()).wait_send()
                if self.by_x(t, k):
                    self.copy(t, 1 - p.x, y, zz, p.c, 3, k, p.at()).wait_send()
                else:
                    self.copy(t, p.x, 1 - y, zz, p.c, 3, k, p.at()).wait_send()

        self.each_y(t, run)
        for k in (1, 2, 3):
            self.pair_copy(t, k, p.c).wait_send()


SIZES = (80, PART, PART, PART)


HALO = 320
COND = 32
TOK = 512
KEYS = HALO + TOK + COND
TILES = ((0, 0), (256, 256))
LOG2E = 1.4426950408889634


def nt(a, b):
    return lax.dot_general(a, b, (((1,), (1,)), ((), ())), preferred_element_type=jnp.float32)


def tn(a, b):
    return lax.dot_general(a, b, (((0,), (0,)), ((), ())), preferred_element_type=jnp.float32)


def nn(a, b):
    return jnp.dot(a, b, preferred_element_type=jnp.float32)


def make_bias(extra, blk, bias):
    row = lax.broadcasted_iota(jnp.int32, (TOK, 1), 0) + blk * TOK
    at = lax.broadcasted_iota(jnp.int32, (1, KEYS), 1)
    key = at + (blk * TOK - HALO)
    item_q, item_k = jnp.zeros_like(row), jnp.zeros_like(key)
    end = 0
    for n in range(extra.shape[1]):
        end = end + extra[0, n] + (LEN_MIN - 1)
        item_q += (row >= end).astype(jnp.int32)
        item_k += (key >= end).astype(jnp.int32)
    item_k = jnp.where(key >= 0, item_k, -1)
    item_k = jnp.where(at >= HALO + TOK, (at - (HALO + TOK)) >> 1, item_k)
    for low in range(0, TOK, 128):
        bias[low : low + 128] = jnp.where(item_q[low : low + 128] == item_k, 0.0, -1e30)


def head(h):
    return slice(HEAD * h, HEAD * (h + 1))


class Names:
    def __init__(self, names, refs):
        for name, ref in zip(names, refs, strict=True):
            setattr(self, name, ref)


def hbm(shape, dtype=jnp.bfloat16):
    return jax.ShapeDtypeStruct(shape, dtype)


GROUP = 4
IN_VMEM = pl.BlockSpec(memory_space=pltpu.VMEM)
IN_SMEM = pl.BlockSpec(memory_space=pltpu.SMEM)
FWD_IN = dict(
    skip_bias=IN_VMEM, first_gain=IN_VMEM, first_shift=IN_VMEM, out_bias=IN_VMEM, second_gain=IN_VMEM,
    second_shift=IN_VMEM, down_bias=IN_VMEM, up_bias=IN_VMEM, extra=IN_SMEM, cond=IN_VMEM, latents=ANY, skip_input=ANY, skip=ANY, joint=ANY, out=ANY, up=ANY, down=ANY,
)
FWD_OUT = dict(
    w_skip=hbm((16, PART, WIDTH)),
    w_joint=hbm((8, PART, 4 * WIDTH)),
    w_up=hbm((8, PART, 4 * WIDTH)),
    w_down=hbm((32, PART, WIDTH)),
    output=hbm((TOK, WIDTH)),
    hidden_t=hbm((8, 4, PART, TOK)),
    slope=hbm((TOK, 4 * WIDTH)),
    second_t=hbm((8, PART, TOK)),
    second_unit=hbm((TOK, WIDTH)),
    att_t=hbm((8, PART, TOK)),
    q=hbm((HEADS, TOK, HEAD)),
    k=hbm((HEADS, KEYS, HEAD)),
    v=hbm((HEADS, KEYS, HEAD)),
    o=hbm((HEADS, TOK, HEAD)),
    logsum=hbm((HEADS, TOK, 1), jnp.float32),
    first_t=hbm((8, PART, TOK)),
    first_unit=hbm((TOK, WIDTH)),
    joined_t=hbm((8, 2 * PART, TOK)),
)
FWD_VM = dict(
    cond_t=hbm((8, PART, 128)),
    second_rstd=hbm((TOK, 1), jnp.float32),
    first_rstd=hbm((TOK, 1), jnp.float32),
    vectors=hbm((16, WIDTH), jnp.float32),
    cond_unit=hbm((COND, WIDTH), jnp.float32),
    cond_rstd=hbm((COND, 1), jnp.float32),
)
FWD_SCRATCH = dict(
    lat=pltpu.VMEM((TOK, WIDTH), jnp.bfloat16),
    ski=pltpu.VMEM((TOK, WIDTH), jnp.bfloat16),
    weight=pltpu.VMEM((2, 8, PART, WIDTH), jnp.bfloat16),
    base=pltpu.VMEM((TOK, WIDTH), jnp.float32),
    acc=pltpu.VMEM((TOK, WIDTH), jnp.float32),
    unit=pltpu.VMEM((TOK, WIDTH), jnp.bfloat16),
    normed=pltpu.VMEM((TOK, WIDTH), jnp.bfloat16),
    pairs=pltpu.VMEM((2, TOK, WIDTH), jnp.bfloat16),
    halo=pltpu.VMEM((2, HALO, WIDTH), jnp.bfloat16),
    cond_in=pltpu.VMEM((COND, WIDTH), jnp.bfloat16),
    qh=pltpu.VMEM((HEADS, TOK, HEAD), jnp.bfloat16),
    kh=pltpu.VMEM((HEADS, KEYS, HEAD), jnp.bfloat16),
    vh=pltpu.VMEM((HEADS, KEYS, HEAD), jnp.bfloat16),
    oh=pltpu.VMEM((HEADS, TOK, HEAD), jnp.bfloat16),
    lh=pltpu.VMEM((HEADS // 2, 256, 1), jnp.float32),
    bias=pltpu.VMEM((TOK, KEYS), jnp.float32),
    hidden=pltpu.VMEM((4, TOK, WIDTH), jnp.bfloat16),
    turned=pltpu.VMEM((2, WIDTH, TOK), jnp.bfloat16),
    tile=pltpu.VMEM((2, TOK, WIDTH), jnp.bfloat16),
    pack=pltpu.VMEM(SMALL, jnp.float32),
    packs=pltpu.VMEM((8, *SMALL), jnp.float32),
    ups=pltpu.VMEM((4, 1, WIDTH), jnp.float32),
    w_sems=pltpu.SemaphoreType.DMA((2,)),
    t_sems=pltpu.SemaphoreType.DMA((24,)),
    halo_sems=pltpu.SemaphoreType.DMA((2, 2)),
)
N_GATHER = len(Gather.SEMS) + len(Gather.STAGE)


def forward_kernel(*refs):
    cuts = [len(FWD_IN), len(FWD_OUT), len(FWD_VM), len(FWD_SCRATCH), N_GATHER]
    pieces, at = [], 0
    for cut in cuts:
        pieces.append(refs[at : at + cut])
        at += cut
    i, o, vm, b = (
        Names(names, part) for names, part in zip((FWD_IN, FWD_OUT, FWD_VM, FWD_SCRATCH), pieces)
    )
    f32, bf16 = jnp.float32, jnp.bfloat16
    p = Place()
    g = Gather(
        p, (b.pack, i.skip, i.joint, i.out, i.up, i.down), (b.packs, o.w_skip, o.w_joint, o.w_up, o.w_down), pieces[4]
    )

    def copy(src, dst, sem):
        return pltpu.make_async_copy(src, dst, sem)

    def stream(blocks, body):
        def load(n):
            return copy(blocks[n], b.weight.at[n % 2], b.w_sems.at[n % 2])

        load(0).start()
        for n in range(len(blocks)):
            if n + 1 < len(blocks):
                load(n + 1).start()
            load(n).wait()
            body(n, b.weight[n % 2].reshape(WIDTH, WIDTH))

    def column(ref, q):
        return ref.at[:, :, pl.ds(q * WIDTH, WIDTH)]

    def by_rows(size, body):
        @pl.loop(0, TOK // size)
        def _(n):
            body(pl.ds(pl.multiple_of(n * size, size), size))

    def vector(n):
        return vm.vectors[n : n + 1, :]

    kept = []

    def keep(src, dst, sem):
        one = (src, dst, b.t_sems.at[sem])
        copy(*one).start()
        kept.append(one)

    def flush():
        for one in kept:
            copy(*one).wait()
        kept.clear()

    def norm(values):
        center = values - jnp.mean(values, axis=1, keepdims=True)
        rstd = lax.rsqrt(jnp.mean(center * center, axis=1, keepdims=True) + 1e-05)
        return center * rstd, rstd

    def norm_tokens(gain, shift, rstd_out):
        @functools.partial(by_rows, 64)
        def _(rows):
            unit, rstd = norm(b.base[rows])
            b.unit[rows] = unit.astype(bf16)
            rstd_out[rows] = rstd
            b.normed[rows] = (unit * gain + shift).astype(bf16)

    def turn(slot, src, dst, sem):
        b.turned[slot] = src.T
        keep(b.turned.at[slot], dst, sem)

    loads = [(i.latents, b.lat, b.t_sems.at[0]), (i.skip_input, b.ski, b.t_sems.at[1])]
    for t in range(4):
        g.own_start(t)
    for one in loads:
        copy(*one).start()
    b.pack[...] = jnp.zeros(SMALL, f32)
    few = (i.skip_bias, i.first_gain, i.first_shift, i.out_bias, i.second_gain, i.second_shift, i.down_bias)
    for n, ref in enumerate(few):
        b.pack[n : n + 1, 0:PART] = ref[...].astype(f32).reshape(1, PART)
    wide = i.up_bias[...].astype(f32).reshape(1, 4 * PART)
    for n in range(4):
        b.pack[7 + n : 8 + n, 0:PART] = wide[:, n * PART : (n + 1) * PART]
    b.packs[p.b] = b.pack[...]
    greet(p)
    g.small_start()
    g.own_done(0)
    g.z_start(0)
    make_bias(i.extra, p.b, b.bias)
    g.small_pass()
    for one in loads:
        copy(*one).wait()

    @pl.when(p.b == 0)
    def _():
        for n in range(HEADS):
            b.kh[n, 0:HALO] = jnp.zeros((HALO, HEAD), bf16)
            b.vh[n, 0:HALO] = jnp.zeros((HALO, HEAD), bf16)

    for k in (1, 2, 3):
        g.z_done(0, k)
        g.xy_start(0, k)
        if k == 2:
            g.own_done(1)
            g.z_start(1)
    g.small_done()
    for n in range(8):
        for row in range(7):
            vm.vectors[row : row + 1, n * PART : (n + 1) * PART] = b.packs[n, row : row + 1, 0:PART]
        for j in range(4):
            at = 4 * n + j
            low = at % 8 * PART
            b.ups[at // 8, :, low : low + PART] = b.packs[n, 7 + j : 8 + j, 0:PART]
    vm.vectors[7:16, :] = jnp.zeros((9, WIDTH), f32)
    for k in (1, 2, 3):
        g.xy_done(0, k)
    g.z_done(1, 1)
    g.xy_start(1, 1)
    for k in (1, 2, 3):
        g.diag_done(0, k)
    g.ready(0)

    def do_base(n, weight):
        made = nn((b.lat, b.ski)[n][...], weight)
        if n == 0:
            b.base[...] = made + vector(0)
        else:
            b.base[...] += made
        if n == 0:
            g.z_done(1, 2)
            g.z_done(1, 3)
            g.xy_start(1, 2)
            g.own_done(2)
            g.z_start(2)

    stream([o.w_skip.at[pl.ds(8 * n, 8)] for n in range(2)], do_base)
    norm_tokens(vector(1), vector(2), vm.first_rstd)
    g.xy_start(1, 3)
    g.z_done(2, 1)
    for n in range(COND // 2):
        vm.cond_unit[2 * n : 2 * n + 2] = i.cond[n].astype(f32)
    unit, rstd = norm(vm.cond_unit[...])
    vm.cond_unit[...] = unit
    vm.cond_rstd[...] = rstd
    cond_in = (unit * vector(1) + vector(2)).astype(bf16)
    b.cond_in[...] = cond_in
    keep(b.unit, o.first_unit, 2)
    for n in range(2):
        b.turned[n] = (b.lat, b.ski)[n][...].T
        made = b.turned.at[n].reshape(8, PART, TOK)
        for k in range(4):
            keep(made.at[pl.ds(2 * k, 2)].reshape(2 * PART, TOK), o.joined_t.at[4 * n + k], 3 + 4 * n + k)
        if n == 0:
            g.z_done(2, 2)
            g.own_done(3)
            g.z_start(3)
    turned = jnp.concatenate([cond_in.astype(f32)] * 2 + [jnp.zeros((128 - 2 * COND, WIDTH), f32)], 0).T
    vm.cond_t[...] = turned.astype(bf16).reshape(8, PART, 128)
    for k in (1, 2, 3):
        g.xy_done(1, k)
    g.xy_start(2, 1)
    g.z_done(2, 3)
    for k in (1, 2, 3):
        g.diag_done(1, k)
    g.xy_start(2, 2)
    g.xy_start(2, 3)
    g.z_done(3, 1)
    g.ready(1)

    def halo_copy(n, device):
        low, size = ((HALO - 64, 64), (0, HALO - 64))[n]
        src, dst = b.pairs.at[:, pl.ds(TOK - HALO + low, size)], b.halo.at[:, pl.ds(low, size)]
        return remote(src, dst, b.halo_sems.at[n, 0], b.halo_sems.at[n, 1], device)

    def halo_heads(n):
        low, size = ((HALO - 64, 64), (0, HALO - 64))[n]

        @pl.when(p.b > 0)
        def _():
            halo_copy(n, (p.s, p.b)).wait_recv()
            for h in range(HEADS):
                b.kh[h, low : low + size] = b.halo[0, low : low + size, head(h)]
                b.vh[h, low : low + size] = b.halo[1, low : low + size, head(h)]

    def do_triple(n, weight):
        made = nn(b.normed[...], weight).astype(bf16)
        if n < 2:
            b.pairs[n] = made
            few = nn(b.cond_in[...], weight).astype(bf16)
            for h in range(HEADS):
                (b.kh, b.vh)[n][h, HALO + TOK :] = few[:, head(h)]
        else:
            b.tile[0] = made
        if n == 1:
            for m in (0, 1):
                pl.when(p.b < 7)(lambda m=m: halo_copy(m, (p.s, p.b + 1)).start())
            g.z_done(3, 2)

    stream([column(o.w_joint, n) for n in (1, 2, 0)], do_triple)
    for h in range(HEADS):
        b.qh[h] = b.tile[0, :, head(h)]
        b.kh[h, HALO : HALO + TOK] = b.pairs[0, :, head(h)]
        b.vh[h, HALO : HALO + TOK] = b.pairs[1, :, head(h)]
    g.z_done(3, 3)
    flush()
    turn(0, b.normed[...], o.first_t.reshape(WIDTH, TOK), 2)

    halo_heads(0)
    keep(b.qh, o.q, 3)

    def logsum_copy(half, start):
        dst = o.logsum.at[pl.ds(start, HEADS // 2), pl.ds(TILES[half][0], 256)]
        return copy(b.lh, dst, b.t_sems.at[6])

    def attend(half, start, before):
        row, low = TILES[half]
        rows, keys = pl.ds(row, 256), pl.ds(low, KEYS - low)
        if before is not None:
            logsum_copy(*before).wait()

        @pl.loop(0, HEADS // 2)
        def _(n):
            h = start + n
            scores = nt(b.qh[h, rows], b.kh[h, keys]) * (HEAD**-0.5 * LOG2E) + b.bias[rows, keys]
            top = jnp.max(scores, axis=1, keepdims=True)
            expo = jnp.exp2(scores - top)
            total = jnp.sum(expo, axis=1, keepdims=True)
            mixed = nn(expo.astype(bf16), b.vh[h, keys])
            b.oh[h, rows] = (mixed / total).astype(bf16)
            b.lh[n] = top + jnp.log2(total)

        logsum_copy(half, start).start()

    attend(1, 0, None)
    for k in (1, 2, 3):
        g.xy_done(2, k)
    g.xy_start(3, 1)
    attend(1, 8, (1, 0))
    halo_heads(1)
    keep(b.kh, o.k, 4)
    keep(b.vh, o.v, 5)
    g.xy_start(3, 2)
    attend(0, 0, (1, 8))
    g.xy_start(3, 3)
    attend(0, 8, (0, 0))
    logsum_copy(0, 8).wait()
    keep(b.oh, o.o, 7)
    for h in range(HEADS):
        b.tile[0, :, head(h)] = b.oh[h]

    def do_out(_, weight):
        b.base[...] += nn(b.tile[0], weight) + vector(3)

    stream([column(o.w_joint, 3)], do_out)
    norm_tokens(vector(4), vector(5), vm.second_rstd)
    flush()
    keep(b.unit, o.second_unit, 2)
    turn(0, b.tile[0], o.att_t.reshape(WIDTH, TOK), 3)
    turn(1, b.normed[...], o.second_t.reshape(WIDTH, TOK), 4)
    for k in (1, 2, 3):
        g.diag_done(2, k)
    for k in (1, 2, 3):
        g.xy_done(3, k)
    g.ready(2)

    flush()
    hidden_t = o.hidden_t.reshape(4, WIDTH, TOK)

    def wide_keep(q):
        slot = q % 2
        return [
            copy(b.turned.at[slot], hidden_t.at[q], b.t_sems.at[8 + slot]),
            copy(b.tile.at[slot], o.slope.at[:, pl.ds(q * WIDTH, WIDTH)], b.t_sems.at[10 + slot]),
        ]

    def do_up(q, weight):
        slot = q % 2
        b.acc[...] = nn(b.normed[...], weight)
        if q >= 2:
            for one in wide_keep(q - 2):
                one.wait()

        @functools.partial(by_rows, 32)
        def _(rows):
            before = b.acc[rows] + b.ups[q]
            inside = 0.5 + 0.5 * lax.erf(before * 2**-0.5)
            bell = jnp.exp2(before * before * (-0.5 * LOG2E)) * 0.3989422804014327
            b.hidden[q, rows] = (before * inside).astype(bf16)
            b.tile[slot, rows] = (inside + before * bell).astype(bf16)

        b.turned[slot] = b.hidden[q].T
        for one in wide_keep(q):
            one.start()
        if q == 1:
            for k in (1, 2, 3):
                g.diag_done(3, k)

    stream([column(o.w_up, q) for q in range(4)], do_up)
    g.ready(3)

    def do_down(q, weight):
        made = nn(b.hidden[q], weight)
        if q == 0:
            b.base[...] += made + vector(6)
        else:
            b.base[...] += made

    stream([o.w_down.at[pl.ds(8 * q, 8)] for q in range(4)], do_down)
    b.normed[...] = b.base[...].astype(bf16)
    keep(b.normed, o.output, 2)
    for q in (2, 3):
        for one in wide_keep(q):
            one.wait()
    flush()
    for m in (0, 1):
        pl.when(p.b < 7)(lambda m=m: halo_copy(m, (p.s, p.b + 1)).wait_send())
    for t in range(4):
        g.all_sent(t)


def forward(arrays):
    vm = pl.BlockSpec(memory_space=pltpu.VMEM)
    outs = pl.pallas_call(
        forward_kernel,
        out_shape=[*FWD_OUT.values(), *FWD_VM.values()],
        in_specs=[*FWD_IN.values()],
        out_specs=[ANY] * len(FWD_OUT) + [vm] * len(FWD_VM),
        scratch_shapes=[*FWD_SCRATCH.values()] + Gather.SEMS + Gather.STAGE,
        compiler_params=pltpu.CompilerParams(collective_id=0, has_side_effects=True, vmem_limit_bytes=60 << 20),
    )(*[arrays[name] for name in FWD_IN])
    return dict(zip([*FWD_OUT, *FWD_VM], outs, strict=True))


ORDER = (0, 2, 1, 3)
UNIT = (PART, WIDTH)


def add_into(out, *ins):
    @pl.loop(0, out.shape[0] // 16)
    def _(i):
        rows = pl.ds(pl.multiple_of(i * 16, 16), 16)
        total = ins[0][rows].astype(jnp.float32)
        for ref in ins[1:]:
            total += ref[rows].astype(jnp.float32)
        out[rows] = total.astype(out.dtype)


class Sum:
    SEMS = [
        pltpu.SemaphoreType.DMA((4, 4, 2, 2)),
        pltpu.SemaphoreType.DMA((4, 4, 2)),
        pltpu.SemaphoreType.DMA((4, 4, 2)),
        pltpu.SemaphoreType.DMA((4, 4, 2)),
        pltpu.SemaphoreType.DMA((23,)),
    ]
    SLOTS = [pltpu.VMEM((23, *UNIT), jnp.bfloat16), pltpu.VMEM((4, *UNIT), jnp.bfloat16)]
    LANDS = [
        jax.ShapeDtypeStruct(lead + (size, WIDTH), jnp.bfloat16)
        for size in SIZES
        for lead in ((4, 2), (4,), (4,))
    ]
    PARTS = [
        jax.ShapeDtypeStruct((8, PART, WIDTH), jnp.bfloat16),
        jax.ShapeDtypeStruct((4, PART, 4 * WIDTH), jnp.bfloat16),
        jax.ShapeDtypeStruct((4, PART, 4 * WIDTH), jnp.bfloat16),
        jax.ShapeDtypeStruct((4, 4, PART, WIDTH), jnp.bfloat16),
    ]

    def __init__(self, place, parts, lands, outs, sems, slots):
        self.place, self.parts, self.outs = place, parts, outs
        self.sem1, self.sem2, self.sem3, self.sem4, self.load_sems = sems
        self.slots, self.fins = slots
        self.land1, self.land2, self.land3 = ([lands[3 * t + i] for t in range(4)] for i in range(3))

    def slot(self, t, i):
        return self.slots.at[i, pl.ds(0, SIZES[t])]

    def fin(self, t):
        return self.fins.at[t, pl.ds(0, SIZES[t])]

    def piece(self, t, zz, x, y):
        ref = self.parts[t]
        if t == 0:
            return ref.at[2 * zz + x, pl.ds(pl.multiple_of(64 * y, 16), 80)]
        if t == 3:
            return ref.at[zz, 2 * y + x]
        return ref.at[zz, :, pl.ds(pl.multiple_of((2 * y + x) * WIDTH, 128), WIDTH)]

    def half(self, t, zz, x, y, j):
        return self.piece(t, zz, x, j) if zz < 2 else self.piece(t, zz, j, y)

    def keep(self, zz):
        return self.place.y if zz < 2 else self.place.x

    def first(self, t, zz, j):
        p = self.place
        device = p.at(x=1 - p.x) if zz < 2 else p.at(y=1 - p.y)
        sems = self.sem1.at[t, zz, j]
        src = self.half(t, zz, 1 - p.x, 1 - p.y, j)
        return remote(src, self.land1[t].at[zz, j], sems.at[0], sems.at[1], device)

    def start(self, t, zzs=ORDER):
        for zz in zzs:
            for j in (0, 1):
                self.first(t, zz, j).start()

    def load(self, t, src, i):
        return pltpu.make_async_copy(src, self.slot(t, i), self.load_sems.at[i])

    def second(self, t, zz):
        p = self.place
        device = p.at(y=1 - p.y) if zz < 2 else p.at(x=1 - p.x)
        sems = self.sem2.at[t, zz]
        return remote(self.slot(t, 2 * zz), self.land2[t].at[zz], sems.at[0], sems.at[1], device)

    def pass_on(self, t, after=None):
        p = self.place
        if after is not None:
            for zz in ORDER:
                self.second(after, zz).wait_send()

        def own(zz):
            return self.load(t, self.half(t, zz, p.x, p.y, 1 - self.keep(zz)), 2 * zz)

        def landed(zz):
            return self.load(t, self.land1[t].at[zz, 1 - self.keep(zz)], 2 * zz + 1)

        for zz in ORDER:
            own(zz).start()
        for zz in ORDER:
            for j in (0, 1):
                self.first(t, zz, j).wait_recv()
            landed(zz).start()
        for zz in ORDER:
            own(zz).wait()
            landed(zz).wait()
            add_into(self.slot(t, 2 * zz), self.slot(t, 2 * zz), self.slot(t, 2 * zz + 1))
            self.second(t, zz).start()

    def third(self, t, zz, slot):
        p = self.place
        return remote(
            self.slot(t, 8 + 3 * zz), self.land3[t].at[slot], self.sem3.at[t, zz, 0], self.sem3.at[t, slot, 1],
            p.at(zz=zz),
        )

    def third_sent(self, t):
        for zz in range(4):
            pl.when(zz != self.place.zz)(lambda zz=zz: self.third(t, zz, self.place.zz).wait_send())

    def to_chip(self, t, after=None):
        p = self.place
        if after is not None:
            self.third_sent(after)

        def load(zz, n):
            keep = self.keep(zz)
            if n == 0:
                src = self.half(t, zz, p.x, p.y, keep)
            else:
                src = self.land1[t].at[zz, keep] if n == 1 else self.land2[t].at[zz]
            return self.load(t, src, 8 + 3 * zz + n)

        for zz in ORDER:
            load(zz, 0).start()
            load(zz, 1).start()
        for zz in ORDER:
            self.second(t, zz).wait_recv()
            load(zz, 2).start()
        for zz in ORDER:
            for n in range(3):
                load(zz, n).wait()
            base = 8 + 3 * zz
            mine = self.slot(t, base)
            add_into(mine, mine, self.slot(t, base + 1), self.slot(t, base + 2))

            @pl.when(zz != p.zz)
            def _():
                self.third(t, zz, p.zz).start()

            @pl.when(zz == p.zz)
            def _():
                add_into(self.fin(t), mine)

    def result(self, t, x, y):
        ref = self.outs[t]
        if KINDS[t] == "cols":
            return ref.at[:, pl.ds(pl.multiple_of((2 * y + x) * WIDTH, 128), WIDTH)]
        if KINDS[t] == "rows":
            return ref.at[pl.ds(pl.multiple_of((2 * y + x) * PART, 16), PART)]
        low, size = (0, 80) if y == 0 else (80, 64)
        return ref.at[pl.ds(pl.multiple_of(x * PART + low, 16), size)]

    def fin_part(self, t, y):
        if KINDS[t] != "half" or y == 0:
            return self.fin(t)
        return self.fins.at[t, pl.ds(16, 64)]

    def each_y(self, t, run):
        if KINDS[t] != "half":
            run(self.place.y)
            return
        for value in (0, 1):
            pl.when(self.place.y == value)(lambda value=value: run(value))

    def share(self, t, y, k):
        p = self.place
        sems = self.sem4.at[t, k]
        if k == 1:
            src, dst, device = self.fin_part(t, y), self.result(t, p.x, y), p.at(x=1 - p.x)
        elif k == 2:
            src, dst, device = self.fin_part(t, y), self.result(t, p.x, y), p.at(y=1 - p.y)
        elif t % 2 == 0:
            src = dst = self.result(t, 1 - p.x, y)
            device = p.at(y=1 - p.y)
        else:
            src = dst = self.result(t, p.x, 1 - y)
            device = p.at(x=1 - p.x)
        return remote(src, dst, sems.at[0], sems.at[1], device)

    def arrived(self, t, y, k):
        p = self.place
        ref = self.result(t, 1 - p.x if k & 1 else p.x, 1 - y if k & 2 else y)
        sems = self.sem4.at[t, k]
        return remote(ref, ref, sems.at[0], sems.at[1], p.at())

    def spread(self, t):
        def run(y):
            for k in (1, 2):
                self.share(t, y, k).start()
            pltpu.make_async_copy(self.fin_part(t, y), self.result(t, self.place.x, y), self.sem4.at[t, 0, 0]).start()

        self.each_y(t, run)

    def spread_on(self, t):
        def run(y):
            self.arrived(t, y, 1 if t % 2 == 0 else 2).wait_recv()
            self.share(t, y, 3).start()

        self.each_y(t, run)

    def finish(self, t):
        p = self.place
        for k in (1, 2, 3):
            ref = self.land3[t].at[p.other(k)]
            remote(ref, ref, self.sem3.at[t, p.zz, 0], self.sem3.at[t, p.other(k), 1], p.at()).wait_recv()
            self.load(t, ref, 19 + k).start()
        for k in (1, 2, 3):
            self.load(t, self.land3[t].at[p.other(k)], 19 + k).wait()
        add_into(self.fin(t), self.fin(t), *[self.slot(t, 19 + k) for k in (1, 2, 3)])
        self.spread(t)

    def done(self, t, last):
        p = self.place
        for zz in range(4):
            for j in (0, 1):
                self.first(t, zz, j).wait_send()
            if last:
                self.second(t, zz).wait_send()
        if last:
            self.third_sent(t)

        def run(y):
            self.arrived(t, y, 2 if t % 2 == 0 else 1).wait_recv()
            self.arrived(t, y, 3).wait_recv()
            for k in (1, 2, 3):
                self.share(t, y, k).wait_send()
            pltpu.make_async_copy(self.fin_part(t, y), self.result(t, self.place.x, y), self.sem4.at[t, 0, 0]).wait()

        self.each_y(t, run)


class Vectors:
    SCRATCH = [
        pltpu.VMEM((8, *SMALL), jnp.float32),
        pltpu.VMEM((4, *SMALL), jnp.float32),
        pltpu.VMEM((4, *SMALL), jnp.float32),
        pltpu.VMEM((4, *SMALL), jnp.float32),
        pltpu.VMEM((4, *SMALL), jnp.float32),
        pltpu.VMEM((4, *SMALL), jnp.float32),
        pltpu.VMEM((COND, WIDTH), jnp.float32),
        pltpu.VMEM((COND, WIDTH), jnp.float32),
        pltpu.VMEM((COND, WIDTH), jnp.float32),
        pltpu.VMEM((4, COND, WIDTH), jnp.float32),
        pltpu.SemaphoreType.DMA((16, 2)),
    ]

    def __init__(self, place, small_out, cond_out, scratch):
        self.place, self.small_out, self.cond_out = place, small_out, cond_out
        self.part, self.pair, self.x_in, self.sum1, self.y_in, self.z_in = scratch[:6]
        self.mine, self.cond_pair, self.cond_sum, self.cond_in = scratch[6:10]
        self.sems = scratch[10]

    def copy(self, i, src, dst, device):
        return remote(src, dst, self.sems.at[i, 0], self.sems.at[i, 1], device)

    def small_pair(self, zz):
        p = self.place
        return self.copy(zz, self.part.at[2 * zz + 1 - p.c], self.pair.at[zz], p.at(c=1 - p.c))

    def pair_start(self):
        for zz in range(4):
            self.small_pair(zz).start()
        self.cond_pair_copy().start()

    def cond_pair_copy(self):
        return self.copy(4, self.mine, self.cond_pair, self.place.at(c=1 - self.place.c))

    def pair_end(self):
        p = self.place
        for zz in range(4):
            self.small_pair(zz).wait()
            self.pair[zz] += self.part[2 * zz + p.c]
        self.cond_pair_copy().wait()
        self.cond_sum[...] = self.mine[...] + self.cond_pair[...]
        self.copy(5, self.pair, self.x_in, p.at(x=1 - p.x)).start()
        for k in (1, 2, 3):
            self.copy(6 + k, self.cond_sum, self.cond_in.at[p.zz], p.at(zz=p.other(k))).start()
        self.cond_in[p.zz] = self.cond_sum[...]

    def run_x(self):
        p = self.place
        self.copy(5, self.pair, self.x_in, p.at(x=1 - p.x)).wait()
        self.sum1[...] = self.pair[...] + self.x_in[...]
        self.copy(6, self.sum1, self.y_in, p.at(y=1 - p.y)).start()

    def run_y(self):
        p = self.place
        self.copy(6, self.sum1, self.y_in, p.at(y=1 - p.y)).wait()
        self.sum1[...] += self.y_in[...]
        for k in (1, 2, 3):
            self.copy(9 + k, self.sum1.at[p.other(k)], self.z_in.at[p.zz], p.at(zz=p.other(k))).start()
        self.z_in[p.zz] = self.sum1[p.zz]

    def run_z(self):
        p = self.place
        for k in (1, 2, 3):
            self.copy(9 + k, self.sum1.at[p.other(k)], self.z_in.at[p.zz], p.at(zz=p.other(k))).wait()
            self.copy(6 + k, self.cond_sum, self.cond_in.at[p.zz], p.at(zz=p.other(k))).wait()
        self.small_out[...] = (self.z_in[0] + self.z_in[1]) + (self.z_in[2] + self.z_in[3])
        cond = (self.cond_in[0] + self.cond_in[1]) + (self.cond_in[2] + self.cond_in[3])
        self.cond_out[...] = cond.astype(jnp.bfloat16)


BACK_IN = dict(
    hidden_t=ANY, slope=ANY, cot=ANY, second_t=ANY, second_unit=ANY, att_t=ANY, q=ANY, k=ANY, v=ANY, o=ANY, logsum=ANY,
    first_t=ANY, first_unit=ANY, joined_t=ANY, w_skip=ANY, w_joint=ANY, w_up=ANY, w_down=ANY, cond_t=ANY,
    second_rstd=IN_VMEM, first_rstd=IN_VMEM, vectors=IN_VMEM, cond_unit=IN_VMEM, cond_rstd=IN_VMEM, extra=IN_SMEM,
)
BACK_OUT = dict(
    d_latents=hbm((TOK, WIDTH)),
    d_skip=hbm((TOK, WIDTH)),
    g_skip=hbm((2 * PART, WIDTH)),
    g_joint=hbm((PART, 4 * WIDTH)),
    g_up=hbm((PART, 4 * WIDTH)),
    g_down=hbm((4 * PART, WIDTH)),
    hidden_t2=hbm((4, 4, PART, TOK)),
    second_t2=hbm((4, PART, TOK)),
    att_t2=hbm((4, PART, TOK)),
    first_t2=hbm((4, PART, TOK)),
    joined_t2=hbm((4, 2 * PART, TOK)),
)
BACK_SCRATCH = dict(
    cot_v=pltpu.VMEM((TOK, WIDTH), jnp.bfloat16),
    cot2=pltpu.VMEM((TOK, WIDTH), jnp.bfloat16),
    wide=pltpu.VMEM((4, TOK, WIDTH), jnp.bfloat16),
    before2=pltpu.VMEM((4, TOK, WIDTH), jnp.bfloat16),
    triple2=pltpu.VMEM((3, TOK, WIDTH), jnp.bfloat16),
    branch=pltpu.VMEM((TOK, WIDTH), jnp.bfloat16),
    branch2=pltpu.VMEM((TOK, WIDTH), jnp.bfloat16),
    base_g=pltpu.VMEM((TOK, WIDTH), jnp.bfloat16),
    base2=pltpu.VMEM((TOK, WIDTH), jnp.bfloat16),
    acc=pltpu.VMEM((TOK, WIDTH), jnp.float32),
    d_middle=pltpu.VMEM((TOK, WIDTH), jnp.float32),
    tile=pltpu.VMEM((TOK, WIDTH), jnp.bfloat16),
    weight=pltpu.VMEM((2, 8, PART, WIDTH), jnp.bfloat16),
    left=pltpu.VMEM((2, 2, 4, PART, TOK), jnp.bfloat16),
    made=pltpu.VMEM((2, 4, PART, WIDTH), jnp.bfloat16),
    heads_g=pltpu.VMEM((HEADS, TOK, HEAD), jnp.bfloat16),
    qh=pltpu.VMEM((GROUP, TOK, HEAD), jnp.bfloat16),
    oh=pltpu.VMEM((GROUP, TOK, HEAD), jnp.bfloat16),
    kh=pltpu.VMEM((GROUP, HALO + TOK + COND, HEAD), jnp.bfloat16),
    vh=pltpu.VMEM((GROUP, HALO + TOK + COND, HEAD), jnp.bfloat16),
    lh=pltpu.VMEM((GROUP, TOK, 1), jnp.float32),
    sum_k=pltpu.VMEM((HALO + TOK + COND, HEAD), jnp.float32),
    sum_v=pltpu.VMEM((HALO + TOK + COND, HEAD), jnp.float32),
    bias=pltpu.VMEM((TOK, HALO + TOK + COND), jnp.float32),
    halo2=pltpu.VMEM((2, HALO, WIDTH), jnp.bfloat16),
    d_cond=pltpu.VMEM((128, 2 * WIDTH), jnp.bfloat16),
    cond_left=pltpu.VMEM((4, PART, 128), jnp.bfloat16),
    sums=pltpu.VMEM((16, WIDTH), jnp.float32),
    wide_sum=pltpu.VMEM((4, 1, WIDTH), jnp.float32),
    w_sems=pltpu.SemaphoreType.DMA((2,)),
    l_sems=pltpu.SemaphoreType.DMA((2, 8)),
    m_sems=pltpu.SemaphoreType.DMA((2,)),
    t_sems=pltpu.SemaphoreType.DMA((8,)),
    sib_sems=pltpu.SemaphoreType.DMA((34, 2)),
)
SUM_SKIP, SUM_GAIN1, SUM_SHIFT1, SUM_OUT, SUM_GAIN2, SUM_SHIFT2, SUM_DOWN, SUM_UP = range(8)


def back_kernel(*refs):
    cuts = [len(BACK_IN), len(BACK_OUT), 2, len(Sum.PARTS), len(Sum.LANDS), len(BACK_SCRATCH), len(Sum.SEMS), 2]
    pieces, at = [], 0
    for cut in cuts:
        pieces.append(refs[at : at + cut])
        at += cut
    i, o, b = Names(BACK_IN, pieces[0]), Names(BACK_OUT, pieces[1]), Names(BACK_SCRATCH, pieces[5])
    p = Place()
    total = Sum(p, pieces[3], pieces[4], (o.g_skip, o.g_joint, o.g_up, o.g_down), pieces[6], pieces[7])
    vectors = Vectors(p, *pieces[2], refs[at:])
    f32, bf16 = jnp.float32, jnp.bfloat16

    def copy(src, dst, sem):
        return pltpu.make_async_copy(src, dst, sem)

    def sib(n, src, dst):
        return remote(src, dst, b.sib_sems.at[n, 0], b.sib_sems.at[n, 1], p.at(c=1 - p.c))

    def halves(n, src, dst):
        return [sib(4 * n + zz, src.at[2 * zz + 1 - p.c], dst.at[zz]) for zz in range(4)]

    left_pairs = (
        (i.hidden_t, o.hidden_t2), (i.second_t, o.second_t2), (i.att_t, o.att_t2), (i.first_t, o.first_t2),
        (i.joined_t, o.joined_t2),
    )

    def column(ref, q):
        return ref.at[:, :, pl.ds(q * WIDTH, WIDTH)]

    blocks = [i.w_down.at[pl.ds(8 * q, 8)] for q in range(4)]
    blocks += [column(i.w_up, q) for q in range(4)]
    blocks += [column(i.w_joint, q) for q in (3, 0, 1, 2)]
    blocks += [i.w_skip.at[pl.ds(8 * n, 8)] for n in range(2)]

    def load_weight(n):
        return copy(blocks[n], b.weight.at[n % 2], b.w_sems.at[n % 2])

    def stream(start, count, body):
        for n in range(start, start + count):
            if n + 1 < len(blocks):
                load_weight(n + 1).start()
            load_weight(n).wait()
            body(n - start, b.weight[n % 2].reshape(WIDTH, WIDTH))

    def by_rows(size, body):
        @pl.loop(0, TOK // size)
        def _(n):
            body(pl.ds(pl.multiple_of(n * size, size), size))

    def add_sum(row, value):
        b.sums[row : row + 1, :] += value

    def colsum(value):
        return jnp.sum(value, axis=0, keepdims=True)

    def form(n, dst, own, own2, pairs, extra=None):
        result = nn(own.reshape(4 * PART, TOK), pairs[0]) + nn(own2.reshape(4 * PART, TOK), pairs[1])
        if extra is not None:
            result += extra
        slot = n % 2
        b.made[slot] = result.astype(bf16).reshape(4, PART, WIDTH)
        copy(b.made.at[slot], dst, b.m_sems.at[slot]).start()

    def formed(n, dst):
        copy(b.made.at[n % 2], dst, b.m_sems.at[n % 2]).wait()

    def send_all(copies):
        for one in copies:
            one.start()

    def recv_all(copies):
        for one in copies:
            one.wait_recv()

    def left_copies(n):
        own, other = b.left.at[n % 2, 0], b.left.at[n % 2, 1]
        sems = b.l_sems.at[n % 2]
        if n < 4:
            zz = ORDER[n]
            pairs = [(i.hidden_t.at[2 * zz + p.c], own), (o.hidden_t2.at[zz], other)]
        elif n < 7:
            src, src2 = left_pairs[n - 3]
            pairs = [(src.at[2 * zz + p.c], own.at[zz]) for zz in range(4)] + [(src2, other)]
        else:
            pairs = []
            for k in range(4):
                zz, rows = 2 * (n - 7) + k // 2, pl.ds((k % 2) * PART, PART)
                pairs.append((i.joined_t.at[2 * zz + p.c, rows], own.at[k]))
                pairs.append((o.joined_t2.at[zz, rows], other.at[k]))
        return [copy(src, dst, sems.at[m]) for m, (src, dst) in enumerate(pairs)]

    def left_start(n):
        if n < 4:
            left_sends[0][ORDER[n]].wait_recv()
        elif n < 7:
            recv_all(left_sends[n - 3])
        else:
            recv_all(left_sends[4][2 * (n - 7) : 2 * (n - 7) + 2])
        send_all(left_copies(n))

    def left_done(n):
        for one in left_copies(n):
            one.wait()
        return b.left[n % 2, 0], b.left[n % 2, 1]

    cot_load = copy(i.cot, b.cot_v, b.t_sems.at[0])
    cot_load.start()
    load_weight(0).start()
    greet(p)
    sib_cot = sib(20, i.cot, b.cot2)
    left_sends = [halves(n, src, dst) for n, (src, dst) in enumerate(left_pairs)]
    send_all([left_sends[0][zz] for zz in ORDER])
    sib_cot.start()
    b.sums[...] = jnp.zeros_like(b.sums)
    b.d_cond[2 * COND :] = jnp.zeros((128 - 2 * COND, 2 * WIDTH), bf16)
    vectors.part[...] = jnp.zeros_like(vectors.part)
    make_bias(i.extra, p.b, b.bias)
    cot_load.wait()

    def before_sib(q):
        return sib(21 + q, b.wide.at[q], b.before2.at[q])

    def slope_load(q):
        return copy(i.slope.at[:, pl.ds(q * WIDTH, WIDTH)], b.tile, b.t_sems.at[1])

    def do_before(q, weight):
        slope_load(q).start()
        b.acc[...] = nt(b.cot_v[...], weight)
        slope_load(q).wait()
        b.wide_sum[q] = jnp.zeros((1, WIDTH), f32)

        @functools.partial(by_rows, 64)
        def _(rows):
            value = (b.acc[rows] * b.tile[rows].astype(f32)).astype(bf16)
            b.wide[q, rows] = value
            b.wide_sum[q] += colsum(value.astype(f32))

        before_sib(q).start()

    stream(0, 4, do_before)

    for n in (1, 2, 3, 4):
        send_all(left_sends[n])

    sib_cot.wait_recv()
    down_parts = pieces[3][3]
    left_start(0)
    for n, zz in enumerate(ORDER):
        left_start(n + 1)
        form(n, down_parts.at[zz], *left_done(n), (b.cot_v[...], b.cot2[...]))
        if n > 0:
            formed(n - 1, down_parts.at[ORDER[n - 1]])
            total.start(3, (ORDER[n - 1],))

    up_parts = pieces[3][2]
    lefts = left_done(4)
    for q in range(4):
        before_sib(q).wait_recv()
        form(q, column(up_parts, q), *lefts, (b.wide[q], b.before2[q]))
        if q == 0:
            formed(3, down_parts.at[ORDER[3]])
            total.start(3, (ORDER[3],))
        else:
            formed(q - 1, column(up_parts, q - 1))
    left_start(5)

    def do_second(q, weight):
        value = nt(b.wide[q], weight)
        if q == 0:
            b.acc[...] = value
        else:
            b.acc[...] += value

    unit_load = copy(i.second_unit, b.tile, b.t_sems.at[1])
    unit_load.start()
    stream(4, 4, do_second)
    unit_load.wait()
    formed(3, column(up_parts, 3))

    def norm_rows(unit, rstd, gain, grad, gain_row, shift_row):
        scaled = grad * gain
        mean1 = jnp.mean(scaled, axis=1, keepdims=True)
        mean2 = jnp.mean(scaled * unit, axis=1, keepdims=True)
        add_sum(gain_row, colsum(grad * unit))
        add_sum(shift_row, colsum(grad))
        return rstd * (scaled - mean1 - unit * mean2)

    @functools.partial(by_rows, 64)
    def _(rows):
        unit = b.tile[rows].astype(f32)
        back = norm_rows(unit, i.second_rstd[rows], i.vectors[4:5], b.acc[rows], SUM_GAIN2, SUM_SHIFT2)
        g = b.cot_v[rows].astype(f32)
        middle = g + back
        b.d_middle[rows] = middle
        low = middle.astype(bf16)
        b.branch[rows] = low
        add_sum(SUM_OUT, colsum(low.astype(f32)))
        add_sum(SUM_DOWN, colsum(g))

    branch_sib = sib(25, b.branch, b.branch2)
    branch_sib.start()
    total.pass_on(3)
    total.start(2)

    def do_attended(_, weight):
        b.tile[...] = nt(b.branch[...], weight).astype(bf16)
        for h in range(HEADS):
            b.heads_g[h] = b.tile[:, head(h)]

    stream(8, 1, do_attended)

    joint_parts = pieces[3][1]
    lefts = left_done(5)
    left_start(6)
    branch_sib.wait_recv()
    form(0, column(joint_parts, 3), *lefts, (b.branch[...], b.branch2[...]))

    formed(0, column(joint_parts, 3))
    for q in range(4):
        before_sib(q).wait_send()

    def halo_copy(n, device):
        low, size = ((0, 512), (512, 256), (768, 384))[n]
        columns = pl.ds(low, size)
        src = b.before2.at[pl.ds(0, 2), pl.ds(0, HALO), columns]
        sems = b.sib_sems.at[31 + n]
        return remote(src, b.halo2.at[:, :, columns], sems.at[0], sems.at[1], device)

    def halo_start(n):
        pl.when(p.b > 0)(lambda: halo_copy(n, (p.s, p.b - 1)).start())

    scale = HEAD**-0.5
    n_keys = HALO + TOK + COND

    def group_loads(start):
        hs = pl.ds(start, GROUP)
        pairs = ((i.q, b.qh), (i.o, b.oh), (i.k, b.kh), (i.v, b.vh), (i.logsum, b.lh))
        return [copy(src.at[hs], dst, b.t_sems.at[n]) for n, (src, dst) in enumerate(pairs)]

    def group(start):
        send_all(group_loads(start))
        for one in group_loads(start):
            one.wait()

        @pl.loop(0, GROUP)
        def _(h):
            for row, low in TILES:
                rows, keys = pl.ds(row, 256), pl.ds(low, n_keys - low)
                q, k, v, g = b.qh[h, rows], b.kh[h, keys], b.vh[h, keys], b.heads_g[start + h, rows]
                scores = nt(q, k) * (scale * LOG2E) + b.bias[rows, keys]
                probs = jnp.exp2(scores - b.lh[h, rows])
                d_probs = nt(g, v)
                inner = jnp.sum(g.astype(f32) * b.oh[h, rows].astype(f32), axis=1, keepdims=True)
                d_scores = (probs * (d_probs - inner)).astype(bf16)
                d_k, d_v = tn(d_scores, q), tn(probs.astype(bf16), g)
                if row == 0:
                    b.sum_k[...] = d_k
                    b.sum_v[...] = d_v
                else:
                    b.sum_k[keys] += d_k
                    b.sum_v[keys] += d_v
                b.oh[h, rows] = (nn(d_scores, k) * scale).astype(bf16)
            b.kh[h] = (b.sum_k[...] * scale).astype(bf16)
            b.vh[h] = b.sum_v[...].astype(bf16)

        for n in range(GROUP):
            at = head(start + n)
            b.wide[0, :, at] = b.oh[n]
            for j, made in ((0, b.kh), (1, b.vh)):
                wide = slice(j * WIDTH + at.start, j * WIDTH + at.stop)
                b.before2[j, 0:HALO, at] = made[n, 0:HALO]
                b.wide[1 + j, :, at] = made[n, HALO : HALO + TOK]
                b.d_cond[0:COND, wide] = made[n, HALO + TOK :]

    group(0)
    group(4)
    halo_start(0)
    group(8)
    halo_start(1)
    group(12)
    halo_start(2)

    cond_sib = sib(30, b.d_cond.at[pl.ds(0, COND)], b.d_cond.at[pl.ds(COND, COND)])
    cond_sib.start()

    def triple_sib(j):
        return sib(26 + j, b.wide.at[j], b.triple2.at[j])

    triple_sib(0).start()
    for zz in range(4):
        copy(i.cond_t.at[2 * zz + p.c], b.cond_left.at[zz], b.t_sems.at[4 + zz]).start()
    unit_load = copy(i.first_unit, b.tile, b.t_sems.at[1])
    unit_load.start()

    def do_first(j, weight):
        if j == 1:
            merge_halo()
        value = nt(b.wide[j], weight)
        if j == 0:
            b.acc[...] = value
        else:
            b.acc[...] += value
            cond = nt(b.d_cond[0:COND, (j - 1) * WIDTH : j * WIDTH], weight)
            if j == 1:
                vectors.mine[...] = cond
            else:
                vectors.mine[...] += cond

    def merge_halo():
        @pl.when(p.b < 7)
        def _():
            for n in range(3):
                halo_copy(n, (p.s, p.b)).wait_recv()

            @pl.loop(0, HALO // 64)
            def _(n):
                low = pl.ds(pl.multiple_of(n * 64, 64), 64)
                rows = pl.ds(pl.multiple_of(n * 64 + TOK - HALO, 64), 64)
                for j in (0, 1):
                    extra = b.halo2[j, low].astype(f32)
                    b.wide[1 + j, rows] = (b.wide[1 + j, rows].astype(f32) + extra).astype(bf16)

        triple_sib(1).start()
        triple_sib(2).start()

    total.pass_on(2, after=3)
    stream(9, 3, do_first)
    total.to_chip(3)
    unit_load.wait()

    @functools.partial(by_rows, 64)
    def _(rows):
        unit = b.tile[rows].astype(f32)
        back = norm_rows(unit, i.first_rstd[rows], i.vectors[1:2], b.acc[rows], SUM_GAIN1, SUM_SHIFT1)
        low = (b.d_middle[rows] + back).astype(bf16)
        b.base_g[rows] = low
        add_sum(SUM_SKIP, colsum(low.astype(f32)))

    base_sib = sib(29, b.base_g, b.base2)
    base_sib.start()
    for zz in range(4):
        copy(i.cond_t.at[2 * zz + p.c], b.cond_left.at[zz], b.t_sems.at[4 + zz]).wait()
    cond_sib.wait_recv()

    lefts = left_done(6)
    left_start(7)
    for j in range(3):
        triple_sib(j).wait_recv()
        extra = None
        if j > 0:
            extra = nn(b.cond_left[...].reshape(4 * PART, 128), b.d_cond[:, (j - 1) * WIDTH : j * WIDTH])
        form(j, column(joint_parts, j), *lefts, (b.wide[j], b.triple2[j]), extra)
        if j > 0:
            formed(j - 1, column(joint_parts, j - 1))
    formed(2, column(joint_parts, 2))
    total.start(1)
    vectors.mine[...] = norm_rows(
        i.cond_unit[...], i.cond_rstd[...], i.vectors[1:2], vectors.mine[...], SUM_GAIN1, SUM_SHIFT1
    )
    for row in range(7):
        for n in range(8):
            vectors.part[n, row : row + 1, 0:PART] = b.sums[row : row + 1, n * PART : (n + 1) * PART]
    for n in range(32):
        row, low = 7 + n % 4, n % 8 * PART
        vectors.part[n // 4, row : row + 1, 0:PART] = b.wide_sum[n // 8, :, low : low + PART]
    vectors.pair_start()

    skip_parts = pieces[3][0]
    base_sib.wait_recv()
    for n in (0, 1):
        lefts = left_done(7 + n)
        if n == 0:
            left_start(8)
        form(n, skip_parts.at[pl.ds(4 * n, 4)], *lefts, (b.base_g[...], b.base2[...]))
    vectors.pair_end()
    total.to_chip(2, after=3)
    for n in (0, 1):
        formed(n, skip_parts.at[pl.ds(4 * n, 4)])

    def do_joined(n, weight):
        made = (b.tile, b.branch)[n]
        made[...] = nt(b.base_g[...], weight).astype(bf16)
        copy(made, (o.d_latents, o.d_skip)[n], b.t_sems.at[n]).start()

    branch_sib.wait_send()
    stream(12, 2, do_joined)
    vectors.run_x()
    total.finish(3)

    total.pass_on(1, after=2)
    total.start(0)
    total.spread_on(3)
    vectors.run_y()
    total.finish(2)
    total.to_chip(1, after=2)
    total.pass_on(0, after=1)
    total.spread_on(2)
    total.finish(1)
    total.to_chip(0, after=1)
    total.spread_on(1)
    total.finish(0)
    total.spread_on(0)
    vectors.run_z()
    for n in (0, 1):
        copy((b.tile, b.branch)[n], (o.d_latents, o.d_skip)[n], b.t_sems.at[n]).wait()
    for group_sends in left_sends:
        for one in group_sends:
            one.wait_send()
    for one in (sib_cot, cond_sib, base_sib, triple_sib(0), triple_sib(1), triple_sib(2)):
        one.wait_send()
    for n in range(3):
        pl.when(p.b > 0)(lambda n=n: halo_copy(n, (p.s, p.b - 1)).wait_send())
    for t in (3, 2, 1, 0):
        total.done(t, t == 0)


def backward(arrays):
    vm = pl.BlockSpec(memory_space=pltpu.VMEM)
    outs = pl.pallas_call(
        back_kernel,
        out_shape=[*BACK_OUT.values()] + [
            jax.ShapeDtypeStruct(SMALL, jnp.float32), jax.ShapeDtypeStruct((COND, WIDTH), jnp.bfloat16)
        ] + Sum.PARTS + Sum.LANDS,
        in_specs=[*BACK_IN.values()],
        out_specs=[ANY] * len(BACK_OUT) + [vm] * 2 + [ANY] * (len(Sum.PARTS) + len(Sum.LANDS)),
        scratch_shapes=[*BACK_SCRATCH.values()] + Sum.SEMS + Sum.SLOTS + Vectors.SCRATCH,
        compiler_params=pltpu.CompilerParams(collective_id=1, has_side_effects=True, vmem_limit_bytes=60 << 20),
    )(*[arrays[name] for name in BACK_IN])
    named = Names(BACK_OUT, outs[: len(BACK_OUT)])
    return named, outs[len(BACK_OUT)], outs[len(BACK_OUT) + 1]


def item_ends(extra_length):
    lengths = extra_length[0] + (LEN_MIN - 1)
    count = lengths.shape[0]
    upto = lax.iota(jnp.int32, count)[None, :] <= lax.iota(jnp.int32, count)[:, None]
    return jnp.sum(jnp.where(upto, lengths[None, :], 0), axis=1)


def quick(
    latents, skip_input, cond_tokens, extra_length, skip_weight, skip_bias, first_gain, first_shift, joint_weight,
    out_weight, out_bias, second_gain, second_shift, up_weight, up_bias, down_weight, down_bias, cotangent,
):
    arrays = dict(
        skip_bias=skip_bias,
        first_gain=first_gain,
        first_shift=first_shift,
        out_bias=out_bias,
        second_gain=second_gain,
        second_shift=second_shift,
        down_bias=down_bias,
        up_bias=up_bias,
        extra=extra_length,
        cond=cond_tokens,
        latents=latents,
        skip_input=skip_input,
        skip=skip_weight.reshape(2, PART, WIDTH),
        joint=joint_weight,
        out=out_weight,
        up=up_weight,
        down=down_weight.reshape(4, PART, WIDTH),
        cot=cotangent,
    )
    made = forward(arrays)
    grads, sums, cond_sum = backward({**arrays, **made})
    return settle(made["output"], grads, sums, cond_sum)


SETTLE_STEPS = 3


def settle_kernel(output, d_latents, d_skip, g_skip, g_joint, g_up, g_down, sums, cond, *outs):
    f32 = jnp.float32
    for src, dst in zip((output, d_latents, d_skip), outs[:3]):
        dst[...] = src[...]
    outs[4][...] = g_skip[...].astype(f32)
    outs[8][...] = g_joint[:, : 3 * WIDTH].astype(f32)
    outs[9][...] = g_joint[:, 3 * WIDTH :].astype(f32)
    outs[13][...] = g_up[...].astype(f32)
    outs[15][...] = g_down[...].astype(f32)

    @pl.when(pl.program_id(0) == 0)
    def _():
        pairs = cond[...].astype(f32)
        for n in range(COND // 2):
            outs[3][n] = pairs[2 * n : 2 * n + 2].astype(jnp.bfloat16)
        for row, n in enumerate((5, 6, 7, 10, 11, 12, 16)):
            outs[n][...] = sums[row : row + 1, 0:PART].reshape(PART)
        wide = jnp.concatenate([sums[7 + n : 8 + n, 0:PART] for n in range(4)], axis=1)
        outs[14][...] = wide.reshape(4 * PART)


def settle(output, grads, sums, cond):
    f32, bf16 = jnp.float32, jnp.bfloat16

    def columns(shape, dtype):
        spec = pl.BlockSpec((shape[0], shape[1] // SETTLE_STEPS), lambda n: (0, n))
        return spec, jax.ShapeDtypeStruct(shape, dtype)

    def rows(shape, dtype):
        spec = pl.BlockSpec((shape[0] // SETTLE_STEPS, shape[1]), lambda n: (n, 0))
        return spec, jax.ShapeDtypeStruct(shape, dtype)

    def whole(shape, dtype):
        spec = pl.BlockSpec(shape, lambda n: (0,) * len(shape))
        return spec, jax.ShapeDtypeStruct(shape, dtype)

    token, few = columns((TOK, WIDTH), bf16), whole((PART,), f32)
    outs = [
        token, token, token, whole((COND // 2, 2, WIDTH), bf16), rows((2 * PART, WIDTH), f32), few, few, few,
        rows((PART, 3 * WIDTH), f32), rows((PART, WIDTH), f32), few, few, few, rows((PART, 4 * WIDTH), f32),
        whole((4 * PART,), f32), rows((4 * PART, WIDTH), f32), few,
    ]
    ins = [
        token, token, token, rows((2 * PART, WIDTH), bf16), rows((PART, 4 * WIDTH), bf16), rows((PART, 4 * WIDTH), bf16),
        rows((4 * PART, WIDTH), bf16), whole(SMALL, f32), whole((COND, WIDTH), bf16),
    ]
    return tuple(
        pl.pallas_call(
            settle_kernel,
            grid=(SETTLE_STEPS,),
            out_shape=[shape for _, shape in outs],
            in_specs=[spec for spec, _ in ins],
            out_specs=[spec for spec, _ in outs],
            compiler_params=pltpu.CompilerParams(vmem_limit_bytes=60 << 20),
        )(
            output, grads.d_latents, grads.d_skip, grads.g_skip, grads.g_joint, grads.g_up, grads.g_down, sums, cond,
        )
    )


def shifted(value, axis, steps):
    count = lax.axis_size(axis)
    leading, last = (max(0, -steps), min(count, count - steps))
    return lax.ppermute(value, axis, [(source, source + steps) for source in range(leading, last)])


def layer_norm(values, gain, shift):
    center = values - jnp.mean(values, axis=-1, keepdims=True)
    spread = jnp.mean(center * center, axis=-1, keepdims=True)
    return center * lax.rsqrt(spread + 1e-05) * gain + shift


def contract_rows(left, right):
    return lax.dot_general(
        left, right, (((0,), (0,)), ((), ())), preferred_element_type=jnp.float32
    )


def contract_cols(left, right):
    return lax.dot_general(
        left, right, (((1,), (1,)), ((), ())), preferred_element_type=jnp.float32
    )


def segment_ids(ends, places):
    inside = jnp.sum((ends[None, :] <= places[:, None]).astype(jnp.int32), axis=1)
    return jnp.where(places >= 0, inside, -1)


def split_heads(block):
    return block.reshape(block.shape[0], HEADS, HEAD).transpose(1, 0, 2)


def merge_heads(block):
    return block.transpose(1, 0, 2).reshape(block.shape[1], HEADS * HEAD)


def masked_scores(query, keys, allowed):
    scores = contract_cols(query, keys) * HEAD ** (-0.5)
    return jnp.where(allowed, scores, -1e30)


def plain(
    latents,
    skip_input,
    cond_tokens,
    extra_length,
    skip_weight,
    skip_bias,
    first_gain,
    first_shift,
    joint_weight,
    out_weight,
    out_bias,
    second_gain,
    second_shift,
    up_weight,
    up_bias,
    down_weight,
    down_bias,
    cotangent,
):
    whole = (
        lax.all_gather(skip_weight, "blk", axis=0, tiled=True),
        lax.all_gather(skip_bias, "blk", axis=0, tiled=True),
        lax.all_gather(first_gain, "blk", axis=0, tiled=True),
        lax.all_gather(first_shift, "blk", axis=0, tiled=True),
        lax.all_gather(joint_weight, "blk", axis=0, tiled=True),
        lax.all_gather(out_weight, "blk", axis=0, tiled=True),
        lax.all_gather(out_bias, "blk", axis=0, tiled=True),
        lax.all_gather(second_gain, "blk", axis=0, tiled=True),
        lax.all_gather(second_shift, "blk", axis=0, tiled=True),
        lax.all_gather(up_weight, "blk", axis=0, tiled=True),
        lax.all_gather(up_bias, "blk", axis=0, tiled=True),
        lax.all_gather(down_weight, "blk", axis=0, tiled=True),
        lax.all_gather(down_bias, "blk", axis=0, tiled=True),
    )
    (
        skip_matrix,
        skip_offset,
        gain_first,
        shift_first,
        joint_matrix,
        out_matrix,
        out_offset,
        gain_second,
        shift_second,
        up_matrix,
        up_offset,
        down_matrix,
        down_offset,
    ) = whole
    rows = latents.shape[0]
    width = latents.shape[1]
    scale = HEAD ** (-0.5)
    joined = jnp.concatenate([latents, skip_input], 1)
    base = jnp.dot(joined, skip_matrix, preferred_element_type=jnp.float32) + skip_offset
    first_in = layer_norm(base, gain_first, shift_first).astype(jnp.bfloat16)
    triple = jnp.dot(first_in, joint_matrix, preferred_element_type=jnp.float32).astype(
        jnp.bfloat16
    )
    query = triple[:, :width]
    pair_here = triple[:, width:]
    pair_left = shifted(pair_here, "blk", 1)
    cond_flat = cond_tokens.reshape(-1, width).astype(jnp.float32)
    cond_in = layer_norm(cond_flat, gain_first, shift_first).astype(jnp.bfloat16)
    cond_pair = jnp.dot(
        cond_in, joint_matrix[:, width:], preferred_element_type=jnp.float32
    ).astype(jnp.bfloat16)
    pairs = jnp.concatenate([pair_left, pair_here, cond_pair], 0)
    ends = item_ends(extra_length)
    here = lax.axis_index("blk")
    places = here * rows + lax.iota(jnp.int32, rows)
    seg_here = segment_ids(ends, places)
    seg_left = segment_ids(ends, places - rows)
    cond_seg = lax.iota(jnp.int32, cond_pair.shape[0]) // 2
    allowed = seg_here[:, None] == jnp.concatenate([seg_left, seg_here, cond_seg])[None, :]
    head_query = split_heads(query)
    head_key = split_heads(pairs[:, :width])
    head_value = split_heads(pairs[:, width:])

    def head_forward(parts):
        query_one, key_one, value_one = parts
        scores = masked_scores(query_one, key_one, allowed)
        top = jnp.max(scores, axis=1, keepdims=True)
        expo = jnp.exp(scores - top)
        total = jnp.sum(expo, axis=1, keepdims=True)
        probs = (expo / total).astype(jnp.bfloat16)
        mixed = jnp.dot(probs, value_one, preferred_element_type=jnp.float32)
        return (mixed, (top + jnp.log(total))[:, 0])

    mixed, logsum = lax.map(head_forward, (head_query, head_key, head_value))
    attended = merge_heads(mixed).astype(jnp.bfloat16)
    middle = base + jnp.dot(attended, out_matrix, preferred_element_type=jnp.float32) + out_offset
    second_in = layer_norm(middle, gain_second, shift_second).astype(jnp.bfloat16)
    before = jnp.dot(second_in, up_matrix, preferred_element_type=jnp.float32) + up_offset
    hidden = jax.nn.gelu(before, approximate=False).astype(jnp.bfloat16)
    output = middle + jnp.dot(hidden, down_matrix, preferred_element_type=jnp.float32) + down_offset
    again = (
        lax.all_gather(skip_weight, "blk", axis=0, tiled=True),
        lax.all_gather(skip_bias, "blk", axis=0, tiled=True),
        lax.all_gather(first_gain, "blk", axis=0, tiled=True),
        lax.all_gather(first_shift, "blk", axis=0, tiled=True),
        lax.all_gather(joint_weight, "blk", axis=0, tiled=True),
        lax.all_gather(out_weight, "blk", axis=0, tiled=True),
        lax.all_gather(out_bias, "blk", axis=0, tiled=True),
        lax.all_gather(second_gain, "blk", axis=0, tiled=True),
        lax.all_gather(second_shift, "blk", axis=0, tiled=True),
        lax.all_gather(up_weight, "blk", axis=0, tiled=True),
        lax.all_gather(up_bias, "blk", axis=0, tiled=True),
        lax.all_gather(down_weight, "blk", axis=0, tiled=True),
        lax.all_gather(down_bias, "blk", axis=0, tiled=True),
    )
    (
        skip_matrix,
        skip_offset,
        gain_first,
        shift_first,
        joint_matrix,
        out_matrix,
        out_offset,
        gain_second,
        shift_second,
        up_matrix,
        up_offset,
        down_matrix,
        down_offset,
    ) = again
    incoming = cotangent.astype(jnp.float32)
    grad_down_offset = jnp.sum(incoming, axis=0)
    grad_down_matrix = contract_rows(hidden, cotangent)
    d_hidden = contract_cols(cotangent, down_matrix)
    gelu_value, gelu_pull = jax.vjp(partial(jax.nn.gelu, approximate=False), before)
    d_before = gelu_pull(d_hidden)[0].astype(jnp.bfloat16)
    grad_up_offset = jnp.sum(d_before.astype(jnp.float32), axis=0)
    grad_up_matrix = contract_rows(second_in, d_before)
    d_second = contract_cols(d_before, up_matrix)
    norm_value, norm_pull = jax.vjp(
        layer_norm, middle, gain_second.astype(jnp.float32), shift_second.astype(jnp.float32)
    )
    d_middle_norm, grad_gain_second, grad_shift_second = norm_pull(d_second)
    d_middle = incoming + d_middle_norm
    d_branch = d_middle.astype(jnp.bfloat16)
    grad_out_offset = jnp.sum(d_branch.astype(jnp.float32), axis=0)
    grad_out_matrix = contract_rows(attended, d_branch)
    d_attended = contract_cols(d_branch, out_matrix).astype(jnp.bfloat16)

    def head_backward(parts):
        query_one, key_one, value_one, grad_one, logsum_one = parts
        scores = masked_scores(query_one, key_one, allowed)
        probs = jnp.exp(scores - logsum_one[:, None])
        d_probs = contract_cols(grad_one, value_one)
        inner = jnp.sum(probs * d_probs, axis=1, keepdims=True)
        d_scores = (probs * (d_probs - inner)).astype(jnp.bfloat16)
        d_query_one = jnp.dot(d_scores, key_one, preferred_element_type=jnp.float32) * scale
        d_key_one = contract_rows(d_scores, query_one) * scale
        d_value_one = contract_rows(probs.astype(jnp.bfloat16), grad_one)
        return (d_query_one, d_key_one, d_value_one)

    d_query_heads, d_key_heads, d_value_heads = lax.map(
        head_backward, (head_query, head_key, head_value, split_heads(d_attended), logsum)
    )
    d_query = merge_heads(d_query_heads)
    d_pairs = jnp.concatenate([merge_heads(d_key_heads), merge_heads(d_value_heads)], 1)
    d_left = d_pairs[:rows]
    d_own = d_pairs[rows : 2 * rows]
    d_cond_part = d_pairs[2 * rows :]
    d_returned = shifted(d_left.astype(jnp.bfloat16), "blk", -1).astype(d_left.dtype)
    d_cond_total = lax.psum(d_cond_part.astype(jnp.bfloat16), "blk")
    d_triple = jnp.concatenate([d_query, d_own + d_returned], 1).astype(jnp.bfloat16)
    leading = (here == 0).astype(jnp.float32)
    cond_term = contract_rows(cond_in, d_cond_total) * leading
    grad_joint_matrix = contract_rows(first_in, d_triple) + jnp.concatenate(
        [jnp.zeros((width, width), jnp.float32), cond_term], 1
    )
    d_first = contract_cols(d_triple, joint_matrix)
    d_cond_in = contract_cols(d_cond_total, joint_matrix[:, width:])
    first_value, first_pull = jax.vjp(
        layer_norm, base, gain_first.astype(jnp.float32), shift_first.astype(jnp.float32)
    )
    d_base_norm, grad_gain_tokens, grad_shift_tokens = first_pull(d_first)
    cond_value, cond_pull = jax.vjp(
        layer_norm, cond_flat, gain_first.astype(jnp.float32), shift_first.astype(jnp.float32)
    )
    d_cond_flat, grad_gain_cond, grad_shift_cond = cond_pull(d_cond_in)
    grad_gain_first = grad_gain_tokens + leading * grad_gain_cond
    grad_shift_first = grad_shift_tokens + leading * grad_shift_cond
    d_base = (d_middle + d_base_norm).astype(jnp.bfloat16)
    grad_skip_offset = jnp.sum(d_base.astype(jnp.float32), axis=0)
    grad_skip_matrix = contract_rows(joined, d_base)
    d_joined = contract_cols(d_base, skip_matrix)
    shares = (
        lax.psum_scatter(
            grad_skip_matrix.astype(jnp.bfloat16), "blk", scatter_dimension=0, tiled=True
        ).astype(jnp.float32),
        lax.psum_scatter(
            grad_skip_offset.astype(jnp.bfloat16), "blk", scatter_dimension=0, tiled=True
        ).astype(jnp.float32),
        lax.psum_scatter(
            grad_gain_first.astype(jnp.bfloat16), "blk", scatter_dimension=0, tiled=True
        ).astype(jnp.float32),
        lax.psum_scatter(
            grad_shift_first.astype(jnp.bfloat16), "blk", scatter_dimension=0, tiled=True
        ).astype(jnp.float32),
        lax.psum_scatter(
            grad_joint_matrix.astype(jnp.bfloat16), "blk", scatter_dimension=0, tiled=True
        ).astype(jnp.float32),
        lax.psum_scatter(
            grad_out_matrix.astype(jnp.bfloat16), "blk", scatter_dimension=0, tiled=True
        ).astype(jnp.float32),
        lax.psum_scatter(
            grad_out_offset.astype(jnp.bfloat16), "blk", scatter_dimension=0, tiled=True
        ).astype(jnp.float32),
        lax.psum_scatter(
            grad_gain_second.astype(jnp.bfloat16), "blk", scatter_dimension=0, tiled=True
        ).astype(jnp.float32),
        lax.psum_scatter(
            grad_shift_second.astype(jnp.bfloat16), "blk", scatter_dimension=0, tiled=True
        ).astype(jnp.float32),
        lax.psum_scatter(
            grad_up_matrix.astype(jnp.bfloat16), "blk", scatter_dimension=0, tiled=True
        ).astype(jnp.float32),
        lax.psum_scatter(
            grad_up_offset.astype(jnp.bfloat16), "blk", scatter_dimension=0, tiled=True
        ).astype(jnp.float32),
        lax.psum_scatter(
            grad_down_matrix.astype(jnp.bfloat16), "blk", scatter_dimension=0, tiled=True
        ).astype(jnp.float32),
        lax.psum_scatter(
            grad_down_offset.astype(jnp.bfloat16), "blk", scatter_dimension=0, tiled=True
        ).astype(jnp.float32),
    )
    (
        share_skip,
        share_skip_offset,
        share_gain_first,
        share_shift_first,
        share_joint,
        share_out,
        share_out_offset,
        share_gain_second,
        share_shift_second,
        share_up,
        share_up_offset,
        share_down,
        share_down_offset,
    ) = shares
    summed = (
        lax.psum(share_skip.astype(jnp.bfloat16), "stream").astype(jnp.float32),
        lax.psum(share_skip_offset.astype(jnp.bfloat16), "stream").astype(jnp.float32),
        lax.psum(share_gain_first.astype(jnp.bfloat16), "stream").astype(jnp.float32),
        lax.psum(share_shift_first.astype(jnp.bfloat16), "stream").astype(jnp.float32),
        lax.psum(share_joint.astype(jnp.bfloat16), "stream").astype(jnp.float32),
        lax.psum(share_out.astype(jnp.bfloat16), "stream").astype(jnp.float32),
        lax.psum(share_out_offset.astype(jnp.bfloat16), "stream").astype(jnp.float32),
        lax.psum(share_gain_second.astype(jnp.bfloat16), "stream").astype(jnp.float32),
        lax.psum(share_shift_second.astype(jnp.bfloat16), "stream").astype(jnp.float32),
        lax.psum(share_up.astype(jnp.bfloat16), "stream").astype(jnp.float32),
        lax.psum(share_up_offset.astype(jnp.bfloat16), "stream").astype(jnp.float32),
        lax.psum(share_down.astype(jnp.bfloat16), "stream").astype(jnp.float32),
        lax.psum(share_down_offset.astype(jnp.bfloat16), "stream").astype(jnp.float32),
    )
    return (
        output.astype(jnp.bfloat16),
        d_joined[:, :width].astype(jnp.bfloat16),
        d_joined[:, width:].astype(jnp.bfloat16),
        d_cond_flat.reshape(cond_tokens.shape).astype(jnp.bfloat16),
        summed[0],
        summed[1],
        summed[2],
        summed[3],
        summed[4],
        summed[5],
        summed[6],
        summed[7],
        summed[8],
        summed[9],
        summed[10],
        summed[11],
        summed[12],
    )


def solution(mesh):
    placed = (
        P(("stream", "blk"), None),
        P(("stream", "blk"), None),
        P("stream", None, None),
        P("stream", None),
        P("blk", None),
        P("blk"),
        P("blk"),
        P("blk"),
        P("blk", None),
        P("blk", None),
        P("blk"),
        P("blk"),
        P("blk"),
        P("blk", None),
        P("blk"),
        P("blk", None),
        P("blk"),
        P(("stream", "blk"), None),
    )
    fits = mesh.shape["stream"] == 4 and mesh.shape["blk"] == 8
    return jax.shard_map(
        quick if fits else plain,
        mesh=mesh,
        in_specs=placed,
        out_specs=(
            P(("stream", "blk"), None),
            P(("stream", "blk"), None),
            P(("stream", "blk"), None),
            P("stream", None, None),
            P("blk", None),
            P("blk"),
            P("blk"),
            P("blk"),
            P("blk", None),
            P("blk", None),
            P("blk"),
            P("blk"),
            P("blk"),
            P("blk", None),
            P("blk"),
            P("blk", None),
            P("blk"),
        ),
        check_vma=False,
    )
```

profile of v0, /device:TPU:12, one launch (start us, length us, event | category | flops | bytes accessed | tf_op | source)
XLA Modules:
  0.0 425.4 jit_solution(15404041800184071214)
XLA Ops:
  0.7 164.4 %shard_map.305 = (bf16[16,144,1152]{2,1,0:T(8,128)(2,1)}, bf16[8,144,4608]{2,1,0:T(8,128)(2,1)}, bf16[8,144,4608]{2,1,0:T(8,128)(2,1)}, bf16[32,144,1152]{2,1,0:...) custom-call(bf16[144]{0:T(256)(128)(2,1)} %refs_0_.1, ...), custom_call_target="tpu_custom_call" | custom-call | tf_op jit(solution)/shard_map/pallas_call | solution.py:717
  165.0 251.3 %shard_map.306 = (bf16[512,1152]{1,0:T(8,128)(2,1)}, bf16[512,1152]{1,0:T(8,128)(2,1)}, bf16[288,1152]{1,0:T(8,128)(2,1)}, bf16[144,4608]{1,0:T(8,128)(2,1)}, bf...) custom-call(bf16[8,4,144,512]{3,2,1,0:T(8,128)(2,1)} %get-tuple-elem, ...), custom_call_target="tpu_custom_call" | custom-call | tf_op jit(solution)/shard_map/pallas_call | solution.py:1514
  416.4 8.7 %shard_map.307 = (bf16[512,1152]{1,0:T(8,128)(2,1)}, bf16[512,1152]{1,0:T(8,128)(2,1)}, bf16[512,1152]{1,0:T(8,128)(2,1)}, bf16[16,2,1152]{2,1,0:T(2,128)(2,1)},...) custom-call(bf16[512,1152]{1,0:T(8,128)(2,1)} %get-tuple-element.49., ...), custom_call_target="tpu_custom_call" | custom-call | tf_op jit(solution)/shard_map/pallas_call | solution.py:1614
where the time goes:
time: 432 us; the launch traced here: 425 us
  Pallas kernels  424 us (98%)
    pallas_call x1, Pallas kernels, backward(): pl.pallas_call(back_kernel, out_shape=[*BACK_OUT.values()] + [jax.ShapeDt...  251 us
    pallas_call x1, Pallas kernels, forward(): pl.pallas_call(forward_kernel, out_shape=[*FWD_OUT.values(), *FWD_VM.valu...  164 us
    pallas_call x1, Pallas kernels, settle(): pl.pallas_call(settle_kernel, grid=(SETTLE_STEPS,), out_shape=[shape for...  8.71 us

commit v1 on v0

--- a/solution.py
+++ b/solution.py
@@ -1419,8 +1419,8 @@
         triple_sib(2).start()
 
     total.pass_on(2, after=3)
+    total.to_chip(3)
     stream(9, 3, do_first)
-    total.to_chip(3)
     unit_load.wait()
 
     @functools.partial(by_rows, 64)

time: 432 us -> 430 us (level)
  no operation moved by 1% of the time
where the time goes in v1:
time: 430 us; the launch traced here: 424 us
  Pallas kernels  424 us (99%)
    pallas_call x1, Pallas kernels, backward(): pl.pallas_call(back_kernel, out_shape=[*BACK_OUT.values()] + [jax.ShapeDt...  250 us
    pallas_call x1, Pallas kernels, forward(): pl.pallas_call(forward_kernel, out_shape=[*FWD_OUT.values(), *FWD_VM.valu...  164 us
    pallas_call x1, Pallas kernels, settle(): pl.pallas_call(settle_kernel, grid=(SETTLE_STEPS,), out_shape=[shape for...  8.71 us

profile of v1, /device:TPU:12, one launch (start us, length us, event | category | flops | bytes accessed | tf_op | source)
XLA Modules:
  0.0 424.4 jit_solution(11473189514057685509)
XLA Ops:
  0.7 164.4 %shard_map.305 = (bf16[16,144,1152]{2,1,0:T(8,128)(2,1)}, bf16[8,144,4608]{2,1,0:T(8,128)(2,1)}, bf16[8,144,4608]{2,1,0:T(8,128)(2,1)}, bf16[32,144,1152]{2,1,0:...) custom-call(bf16[144]{0:T(256)(128)(2,1)} %refs_0_.1, ...), custom_call_target="tpu_custom_call" | custom-call | tf_op jit(solution)/shard_map/pallas_call | solution.py:717
  165.0 250.4 %shard_map.306 = (bf16[512,1152]{1,0:T(8,128)(2,1)}, bf16[512,1152]{1,0:T(8,128)(2,1)}, bf16[288,1152]{1,0:T(8,128)(2,1)}, bf16[144,4608]{1,0:T(8,128)(2,1)}, bf...) custom-call(bf16[8,4,144,512]{3,2,1,0:T(8,128)(2,1)} %get-tuple-elem, ...), custom_call_target="tpu_custom_call" | custom-call | tf_op jit(solution)/shard_map/pallas_call | solution.py:1514
  415.5 8.7 %shard_map.307 = (bf16[512,1152]{1,0:T(8,128)(2,1)}, bf16[512,1152]{1,0:T(8,128)(2,1)}, bf16[512,1152]{1,0:T(8,128)(2,1)}, bf16[16,2,1152]{2,1,0:T(2,128)(2,1)},...) custom-call(bf16[512,1152]{1,0:T(8,128)(2,1)} %get-tuple-element.49., ...), custom_call_target="tpu_custom_call" | custom-call | tf_op jit(solution)/shard_map/pallas_call | solution.py:1614
